TPU v7x, 32 devices: a whole 2x2x4 slice. The times are simulated.
32 devices in a mesh: dp: 4 (over y, x), expert: 4 (over z), tensor: 2 (over core).
Axes of the slice: x: 2, y: 2, z: 4, core: 2. Of those that a mesh axis runs over, the one named last changes fastest.
Arguments:
- tokens: bfloat16 [448, 4096], P(('dp', 'expert'), 'tensor'), may hold values from -6 to 6
- route_ids: int32 [448, 2], P(('dp', 'expert')), may hold values from 0 to 3, all different within a row; in each aligned block of 28 rows (0 to 27, 28 to 55, ...) at most 17 rows name the same one
- route_gates: float32 [448, 2], P(('dp', 'expert')), may hold values from 0.2 to 1
- d_out: bfloat16 [448, 4096], P(('dp', 'expert'), 'tensor'), may hold values from -6 to 6
- gate_saved: bfloat16 [4, 4096, 8192], P(None, 'tensor', ('dp', 'expert')), may hold values from -0.09375 to 0.09375
- up_saved: bfloat16 [4, 4096, 8192], P(None, 'tensor', ('dp', 'expert')), may hold values from -0.09375 to 0.09375
- down_saved: bfloat16 [4, 4096, 8192], P(None, 'tensor', ('dp', 'expert')), may hold values from -0.0625 to 0.0625
Outputs:
- out: bfloat16 [448, 4096], P(('dp', 'expert'), 'tensor')
- d_tokens: bfloat16 [448, 4096], P(('dp', 'expert'), 'tensor')
- grad_gate: bfloat16 [4, 4096, 8192], P('expert', 'tensor', 'dp')
- grad_up: bfloat16 [4, 4096, 8192], P('expert', 'tensor', 'dp')
- grad_down: bfloat16 [4, 4096, 8192], P('expert', 'tensor', 'dp')
Inputs may be any that keep to these rules, and one draw needn't show every extreme that they name: `route_ids`: each token names two different experts. Among the 28 tokens of one aligned block of the token dimension no expert is named more than 17 times, and in some block one expert is named exactly 17 times.
All inputs are finite; a program needn't handle non-finite values.
Results may differ from a plain program's by a relative error of at most 0.028.
Values may be sent and summed in bfloat16 or wider, within the bound.
A program may use at most 128 MiB of HBM per device.

v0:
```python
import jax
import jax.numpy as jnp
from jax import lax
from jax.sharding import PartitionSpec as P


def swiglu_pair(gate_sum, up_sum, back_sum):
    sigmoid_gate = jax.nn.sigmoid(gate_sum)
    silu_gate = gate_sum * sigmoid_gate
    hidden = (silu_gate * up_sum).astype(jnp.bfloat16)
    d_up = (back_sum * silu_gate).astype(jnp.bfloat16)
    d_gate = (back_sum * up_sum * sigmoid_gate * (1.0 + gate_sum * (1.0 - sigmoid_gate))).astype(
        jnp.bfloat16
    )
    return (hidden, d_gate, d_up)


def contract_rows(left_side, right_side):
    return lax.dot_general(
        left_side, right_side, (((0,), (0,)), ((), ())), preferred_element_type=jnp.float32
    )


def contract_last(left_side, right_side):
    return lax.dot_general(
        left_side, right_side, (((1,), (1,)), ((), ())), preferred_element_type=jnp.float32
    )


def spread_back(weights, values):
    return lax.dot_general(
        weights,
        values,
        (((0,), (0,)), ((), ())),
        precision=lax.Precision.HIGHEST,
        preferred_element_type=jnp.float32,
    )


def local(tokens, route_ids, route_gates, d_out, gate_saved, up_saved, down_saved):
    relaid = (
        lax.all_to_all(gate_saved, "expert", split_axis=0, concat_axis=2, tiled=True),
        lax.all_to_all(up_saved, "expert", split_axis=0, concat_axis=2, tiled=True),
        lax.all_to_all(down_saved, "expert", split_axis=0, concat_axis=2, tiled=True),
    )
    w_gate = relaid[0][0]
    w_up = relaid[1][0]
    w_down = relaid[2][0]
    experts = lax.axis_size("expert")
    tok_count = tokens.shape[0]
    capacity = 5 * tok_count // 8
    feature_width = tokens.shape[1]
    onehot = (route_ids[:, :, None] == jnp.arange(experts, dtype=jnp.int32)).astype(jnp.int32)
    flat_hits = onehot.reshape(tok_count * 2, experts)
    before = jnp.cumsum(flat_hits, axis=0) - flat_hits
    slot_index = jnp.sum(before * flat_hits, axis=1).reshape(tok_count, 2)
    target = route_ids * capacity + slot_index
    matches = jnp.arange(experts * capacity, dtype=jnp.int32)[:, None, None] == target[None]
    placer = jnp.sum(matches.astype(jnp.float32), axis=2)
    weighted = jnp.sum(jnp.where(matches, route_gates[None], 0.0), axis=2)
    send_rows = jnp.dot(placer.astype(jnp.bfloat16), tokens, preferred_element_type=jnp.float32)
    send_rows = send_rows.astype(jnp.bfloat16).reshape(experts, capacity, feature_width)
    send_grads = jnp.dot(
        weighted,
        d_out.astype(jnp.float32),
        precision=lax.Precision.HIGHEST,
        preferred_element_type=jnp.float32,
    )
    send_grads = send_grads.astype(jnp.bfloat16).reshape(experts, capacity, feature_width)
    arrived = (
        lax.all_to_all(send_rows, "expert", split_axis=0, concat_axis=0, tiled=True),
        lax.all_to_all(send_grads, "expert", split_axis=0, concat_axis=0, tiled=True),
    )
    collected = (
        lax.all_gather(arrived[0], "dp", axis=0, tiled=True),
        lax.all_gather(arrived[1], "dp", axis=0, tiled=True),
    )
    rows_x = collected[0].reshape(-1, feature_width)
    rows_dy = collected[1].reshape(-1, feature_width)
    gate_part = jnp.dot(rows_x, w_gate, preferred_element_type=jnp.float32)
    up_part = jnp.dot(rows_x, w_up, preferred_element_type=jnp.float32)
    back_part = jnp.dot(rows_dy, w_down, preferred_element_type=jnp.float32)
    summed = (
        lax.psum(gate_part.astype(jnp.bfloat16), "tensor").astype(jnp.float32),
        lax.psum(up_part.astype(jnp.bfloat16), "tensor").astype(jnp.float32),
        lax.psum(back_part.astype(jnp.bfloat16), "tensor").astype(jnp.float32),
    )
    hidden, d_gate, d_up = swiglu_pair(summed[0], summed[1], summed[2])
    out_part = contract_last(hidden, w_down)
    dx_part = contract_last(d_gate, w_gate) + contract_last(d_up, w_up)
    own_sums = (
        lax.psum_scatter(
            out_part.astype(jnp.bfloat16), "dp", scatter_dimension=0, tiled=True
        ).astype(jnp.float32),
        lax.psum_scatter(
            dx_part.astype(jnp.bfloat16), "dp", scatter_dimension=0, tiled=True
        ).astype(jnp.float32),
    )
    grad_gate = contract_rows(rows_x, d_gate).astype(jnp.bfloat16)[None]
    grad_up = contract_rows(rows_x, d_up).astype(jnp.bfloat16)[None]
    grad_down = contract_rows(rows_dy, hidden).astype(jnp.bfloat16)[None]
    back_rows = own_sums[0].astype(jnp.bfloat16).reshape(experts, capacity, feature_width)
    back_grads = own_sums[1].astype(jnp.bfloat16).reshape(experts, capacity, feature_width)
    returned = (
        lax.all_to_all(back_rows, "expert", split_axis=0, concat_axis=0, tiled=True),
        lax.all_to_all(back_grads, "expert", split_axis=0, concat_axis=0, tiled=True),
    )
    result_rows = returned[0].reshape(experts * capacity, feature_width).astype(jnp.float32)
    result_grads = returned[1].reshape(experts * capacity, feature_width).astype(jnp.float32)
    out = spread_back(weighted, result_rows).astype(jnp.bfloat16)
    d_tokens = spread_back(placer, result_grads).astype(jnp.bfloat16)
    return (out, d_tokens, grad_gate, grad_up, grad_down)


def solution(mesh):
    in_specs = (
        P(("dp", "expert"), "tensor"),
        P(("dp", "expert"), None),
        P(("dp", "expert"), None),
        P(("dp", "expert"), "tensor"),
        P(None, "tensor", ("dp", "expert")),
        P(None, "tensor", ("dp", "expert")),
        P(None, "tensor", ("dp", "expert")),
    )
    out_specs = (
        P(("dp", "expert"), "tensor"),
        P(("dp", "expert"), "tensor"),
        P("expert", "tensor", "dp"),
        P("expert", "tensor", "dp"),
        P("expert", "tensor", "dp"),
    )
    return jax.shard_map(local, mesh=mesh, in_specs=in_specs, out_specs=out_specs, check_vma=False)
```

profile of v0, /device:TPU:0, one launch (start us, length us, event | category | flops | bytes accessed | tf_op | source)
XLA Modules:
  0.0 768.0 jit_solution(7553332068043434447)
XLA Ops:
  7.2 0.8 copy.37
  8.0 0.1 eq.30
  8.1 0.1 fusion.12
  8.2 0.1 reduce_window_sum.11
  8.3 0.2 select_reduce_fusion.1
  8.5 0.1 reshape.46
  8.6 0.1 copy.38
  8.7 0.7 multiply_add_fusion
  9.3 0.1 copy.39
  9.4 0.8 copy.40
  10.2 0.1 convert_reduce_fusion
  10.4 0.3 convolution_convert_fusion.5
  10.6 0.8 reshape.47
  11.5 6.3 all-to-all-start
  17.8 0.4 convolution_convert_fusion.4
  18.2 0.8 reshape.51
  19.1 10.4 %all-to-all-done = bf16[4,17,2048]{2,1,0:T(8,128)(2,1)S(1)} async-done(((bf16[4,17,2048]{2,1,0:T(8,128)(2,1)}), bf16[4,17,2048]{2,1,0:T(8,128)(2,1)S(1)}, u32[]{:S(2)}, u32[]{:S(2)}) %all-to-all-start) | async-done | bytes 278560 | tf_op jit(solution)/shard_map/all_to_all | solution.py:71
  29.5 3.5 all-to-all-start.5
  33.0 11.3 %copy.42 = bf16[4,2048,512]{1,2,0:T(8,128)(2,1)} copy(bf16[4,2048,512]{2,1,0:T(8,128)(2,1)} %param.12) | data formatting | bytes 16777216 | tf_op args[5]
  44.3 0.8 copy-done.3
  45.1 5.6 all-to-all-start.2
  50.7 11.3 %copy.41 = bf16[4,2048,512]{1,2,0:T(8,128)(2,1)} copy(bf16[4,2048,512]{2,1,0:T(8,128)(2,1)} %param.11) | data formatting | bytes 16777216 | tf_op args[4]
  62.0 171.0 %all-to-all-done.2 = bf16[4,2048,512]{1,2,0:T(8,128)(2,1)} async-done(((bf16[4,2048,512]{1,2,0:T(8,128)(2,1)}), bf16[4,2048,512]{1,2,0:T(8,128)(2,1)}, u32[]{:S(2)}, u32[]{:S(2)}) %all-to-all-start.2) | async-done | bytes 8388640 | tf_op jit(solution)/shard_map/all_to_all | solution.py:43
  233.0 5.7 all-to-all-start.1
  238.7 11.3 %copy.43 = bf16[4,2048,512]{1,2,0:T(8,128)(2,1)} copy(bf16[4,2048,512]{2,1,0:T(8,128)(2,1)} %param.13) | data formatting | bytes 16777216 | tf_op args[6]
  250.0 171.2 %all-to-all-done.1 = bf16[4,2048,512]{1,2,0:T(8,128)(2,1)} async-done(((bf16[4,2048,512]{1,2,0:T(8,128)(2,1)}), bf16[4,2048,512]{1,2,0:T(8,128)(2,1)}, u32[]{:S(2)}, u32[]{:S(2)}) %all-to-all-start.1) | async-done | bytes 8388640 | tf_op jit(solution)/shard_map/all_to_all | solution.py:42
  421.3 5.6 all-to-all-start.3
  426.9 0.0 all-gather.3.cloned.1.call-start
  427.0 0.7 all-gather.3.cloned.1.call-update
  427.7 0.7 all-gather.5.cloned.1.call-update
  428.4 0.0 all-reduce.8.cloned.1.call-start
  428.5 34.1 %all-gather.3.cloned.1.call-done = bf16[16,17,2048]{2,1,0:T(8,128)(2,1)} async-done(((bf16[4,17,2048]{2,1,0:T(8,128)(2,1)}), bf16[16,17,2048]{2,1,0:T(8,128)(2,1)}) %all-gather.3.cloned.1.call-update) | async-done | bytes 1114128 | tf_op jit(solution)/shard_map/all_gather | solution.py:75
  462.6 1.6 reshape.48
  464.2 31.2 %all-gather.5.cloned.1.call-done = bf16[16,17,2048]{2,1,0:T(8,128)(2,1)} async-done(((bf16[4,17,2048]{2,1,0:T(8,128)(2,1)}), bf16[16,17,2048]{2,1,0:T(8,128)(2,1)}) %all-gather.5.cloned.1.call-update) | async-done | bytes 1114128 | tf_op jit(solution)/shard_map/all_gather | solution.py:76
  495.4 1.8 reshape.52
  497.2 6.9 convolution_convert_fusion.2
  504.1 6.9 convolution_convert_fusion.3
  511.0 98.5 %all-to-all-done.3 = bf16[4,2048,512]{1,2,0:T(8,128)(2,1)} async-done(((bf16[4,2048,512]{1,2,0:T(8,128)(2,1)}), bf16[4,2048,512]{1,2,0:T(8,128)(2,1)}, u32[]{:S(2)}, u32[]{:S(2)}) %all-to-all-start.3) | async-done | bytes 8388640 | tf_op jit(solution)/shard_map/all_to_all | solution.py:44
  609.5 6.9 convolution_convert_fusion
  616.4 0.6 copy-done.6
  617.0 0.6 dynamic-slice.6
  618.3 21.2 %all-reduce.8.cloned.1.call-done = (bf16[272,2048]{1,0:T(8,128)(2,1)}, bf16[272,2048]{1,0:T(8,128)(2,1)}, bf16[272,2048]{1,0:T(8,128)(2,1)}) async-done(((bf16[272,2048]{1,0:T(8,128)(2,1)}, bf16[272,2048]{1,0:T(8,128)(2,1)}, bf16[272,2048]{1,0:T(8,128)(2,1)}), (bf16[272,2048]{1,0:T(8,128)(2,1)}, bf16[272,2048]{1,0:T(8,128)(2,1)}, bf16[272,2048]{1,0:T(8,128)(2,1)})) %all-reduce.8.cloned.1.call-update) | async-done | bytes 3342352 | tf_op jit(solution)/shard_map/psum | solution.py:85
  639.4 7.9 %convolution_convert_fusion.1 = bf16[272,2048]{1,0:T(8,128)(2,1)} fusion(bf16[2048,2048]{0,1:T(8,128)(2,1)} %bitcast.8, bf16[272,2048]{1,0:T(8,128)(2,1)} %get-tuple-element.7, bf16[272,2048]{1,0:T(8,128)(2,1)} %get-tuple-element.8), kind=kOutput, calls=%fused_computation.12 | convolution fusion | flops 2286714880 | bytes 11730944 | tf_op jit(solution)/shard_map/dot_general | solution.py:25
  647.3 6.4 fusion.19
  653.8 7.4 fusion.2
  661.2 48.9 %fusion.21 = (bf16[80,2048]{1,0:T(8,128)(2,1)S(1)}, bf16[80,2048]{1,0:T(8,128)(2,1)S(1)}) fusion(bf16[272,2048]{1,0:T(8,128)(2,1)} %convolution_convert_fusion.1, bf16[272,2048]{1,0:T(8,128)(2,1)} %fusion.2), kind=kCustom, calls=%all-reduce-scatter.2 | all-reduce-scatter fusion | flops 1310721 | bytes 2884096
  710.1 3.3 collective-permute-start
  713.4 10.4 %convert_bitcast_fusion.2 = bf16[1,2048,2048]{2,1,0:T(8,128)(2,1)} fusion(bf16[272,2048]{1,0:T(8,128)(2,1)} %copy-done.4, bf16[272,2048]{1,0:T(8,128)(2,1)} %get-tuple-element.7, bf16[272,2048]{1,0:T(8,128)(2,1)} %get-tuple-element.9, bf16[272,2048]{1,0:T(8,128)(2,1)} %get-tuple-element.8), kind=kOutput, calls=%fused_computation.2 | convolution fusion | flops 2293137408 | bytes 12845056 | tf_op jit(solution)/shard_map/dot_general | solution.py:19
  723.9 3.4 collective-permute-start.1
  727.3 0.7 concatenate
  728.0 0.1 constant_dynamic-slice_fusion.1
  728.1 0.8 reshape.49
  728.9 4.6 all-to-all-start.4
  733.5 10.0 %convert_bitcast_fusion.1 = bf16[1,2048,2048]{2,1,0:T(8,128)(2,1)} fusion(bf16[272,2048]{1,0:T(8,128)(2,1)} %copy-done.4, bf16[272,2048]{1,0:T(8,128)(2,1)} %get-tuple-element.9, bf16[272,2048]{1,0:T(8,128)(2,1)} %get-tuple-element.8), kind=kOutput, calls=%fused_computation.1 | convolution fusion | flops 2290352128 | bytes 11730944 | tf_op jit(solution)/shard_map/dot_general | solution.py:19
  743.5 0.7 concatenate.1
  744.2 0.1 constant_dynamic-slice_fusion
  744.3 0.8 reshape.53
  745.1 5.1 all-to-all-start.6
  750.2 8.7 %convert_bitcast_fusion = bf16[1,2048,2048]{2,1,0:T(8,128)(2,1)} fusion(bf16[272,2048]{1,0:T(8,128)(2,1)S(1)} %reshape.52, bf16[272,2048]{1,0:T(8,128)(2,1)} %get-tuple-element.7, bf16[272,2048]{1,0:T(8,128)(2,1)} %get-tuple-element.8), kind=kOutput, calls=%fused_computation | convolution fusion | flops 2290352128 | bytes 11730944 | tf_op jit(solution)/shard_map/dot_general | solution.py:19
  758.9 0.1 reshape.50
  759.0 0.9 convolution_convert_fusion.7
  759.9 0.5 all-to-all-done.6
  760.4 0.1 reshape.54
  760.5 0.9 convolution_convert_fusion.6
  (26 shorter events, 0.2 us)
Async XLA Ops:
  7.2 3.2 copy-start
  7.2 10.6 %copy-start.5 = (bf16[28,2048]{1,0:T(8,128)(2,1)S(1)}, bf16[28,2048]{1,0:T(8,128)(2,1)}, u32[]{:S(2)}) copy-start(bf16[28,2048]{1,0:T(8,128)(2,1)} %param.10) | copy-start | bytes 344068
  11.5 18.0 %all-to-all-start = ((bf16[4,17,2048]{2,1,0:T(8,128)(2,1)}), bf16[4,17,2048]{2,1,0:T(8,128)(2,1)S(1)}, u32[]{:S(2)}, u32[]{:S(2)}) async-start(bf16[4,17,2048]{2,1,0:T(8,128)(2,1)} %reshape.47), calls=%async_computation | async-start | bytes 786432 | tf_op jit(solution)/shard_map/all_to_all | solution.py:71
  29.5 14.8 %copy-start.2 = (bf16[4,17,2048]{2,1,0:T(8,128)(2,1)}, bf16[4,17,2048]{2,1,0:T(8,128)(2,1)S(1)}, u32[]{:S(2)}) copy-start(bf16[4,17,2048]{2,1,0:T(8,128)(2,1)S(1)} %all-to-all-done) | copy-start | bytes 835588
  29.5 14.8 %all-to-all-start.5 = ((bf16[4,17,2048]{2,1,0:T(8,128)(2,1)}), bf16[4,17,2048]{2,1,0:T(8,128)(2,1)S(1)}, u32[]{:S(2)}, u32[]{:S(2)}) async-start(bf16[4,17,2048]{2,1,0:T(8,128)(2,1)} %reshape.51), calls=%async_computation.5 | async-start | bytes 786432 | tf_op jit(solution)/shard_map/all_to_all | solution.py:72
  44.3 0.8 copy-start.3
  45.1 187.9 %all-to-all-start.2 = ((bf16[4,2048,512]{1,2,0:T(8,128)(2,1)}), bf16[4,2048,512]{1,2,0:T(8,128)(2,1)}, u32[]{:S(2)}, u32[]{:S(2)}) async-start(bf16[4,2048,512]{1,2,0:T(8,128)(2,1)} %copy.42), calls=%async_computation.2 | async-start | bytes 16777216 | tf_op jit(solution)/shard_map/all_to_all | solution.py:43
  233.0 188.3 %all-to-all-start.1 = ((bf16[4,2048,512]{1,2,0:T(8,128)(2,1)}), bf16[4,2048,512]{1,2,0:T(8,128)(2,1)}, u32[]{:S(2)}, u32[]{:S(2)}) async-start(bf16[4,2048,512]{1,2,0:T(8,128)(2,1)} %copy.41), calls=%async_computation.1 | async-start | bytes 16777216 | tf_op jit(solution)/shard_map/all_to_all | solution.py:42
  421.3 188.2 %all-to-all-start.3 = ((bf16[4,2048,512]{1,2,0:T(8,128)(2,1)}), bf16[4,2048,512]{1,2,0:T(8,128)(2,1)}, u32[]{:S(2)}, u32[]{:S(2)}) async-start(bf16[4,2048,512]{1,2,0:T(8,128)(2,1)} %copy.43), calls=%async_computation.3 | async-start | bytes 16777216 | tf_op jit(solution)/shard_map/all_to_all | solution.py:44
  426.9 35.7 %all-gather.3.cloned.1.call-start = ((), (), s32[]{:S(2)}) async-start(), calls=%async_computation.7 | async-start | bytes 1966080 | tf_op jit(solution)/shard_map/all_gather | solution.py:75
  427.7 67.8 %all-gather.5.cloned.1.call-start = ((), (), s32[]{:S(2)}) async-start(), calls=%async_computation.8 | async-start | bytes 1966080 | tf_op jit(solution)/shard_map/all_gather | solution.py:76
  428.4 211.0 %all-reduce.8.cloned.1.call-start = ((), (), s32[]{:S(2)}) async-start(), calls=%async_computation.9 | async-start | bytes 6684672 | tf_op jit(solution)/shard_map/psum | solution.py:85
  464.2 39.9 %copy-start.4 = (bf16[272,2048]{1,0:T(8,128)(2,1)}, bf16[272,2048]{1,0:T(8,128)(2,1)S(1)}, u32[]{:S(2)}) copy-start(bf16[272,2048]{1,0:T(8,128)(2,1)S(1)} %reshape.48) | copy-start | bytes 3342340
  616.4 0.7 copy-start.6
  639.4 7.9 %copy-start.7 = (bf16[272,2048]{1,0:T(8,128)(2,1)S(1)}, bf16[272,2048]{1,0:T(8,128)(2,1)}, u32[]{:S(2)}) copy-start(bf16[272,2048]{1,0:T(8,128)(2,1)} %get-tuple-element.7) | copy-start | bytes 3342340
  639.4 7.9 %copy-start.8 = (bf16[272,2048]{1,0:T(8,128)(2,1)S(1)}, bf16[272,2048]{1,0:T(8,128)(2,1)}, u32[]{:S(2)}) copy-start(bf16[272,2048]{1,0:T(8,128)(2,1)} %get-tuple-element.8) | copy-start | bytes 3342340
  639.4 7.9 %copy-start.9 = (bf16[272,2048]{1,0:T(8,128)(2,1)S(1)}, bf16[272,2048]{1,0:T(8,128)(2,1)}, u32[]{:S(2)}) copy-start(bf16[272,2048]{1,0:T(8,128)(2,1)} %get-tuple-element.9) | copy-start | bytes 3342340
  710.1 17.2 %collective-permute-start = (bf16[36,2048]{1,0:T(8,128)(2,1)S(1)}, bf16[36,2048]{1,0:T(8,128)(2,1)S(1)}, u32[]{:S(2)}, u32[]{:S(2)}) collective-permute-start(bf16[36,2048]{1,0:T(8,128)(2,1)S(1)} %slice), channel_id=1, source_target_pairs={{0,8},{8,16},{16,24},{1,9},{9,17},{17,25},{2,10},{10,18},{18,26},{... | collective-permute-start | bytes 442376
  723.9 19.6 %collective-permute-start.1 = (bf16[36,2048]{1,0:T(8,128)(2,1)S(1)}, bf16[36,2048]{1,0:T(8,128)(2,1)S(1)}, u32[]{:S(2)}, u32[]{:S(2)}) collective-permute-start(bf16[36,2048]{1,0:T(8,128)(2,1)S(1)} %slice.1), channel_id=1, source_target_pairs={{0,8},{8,16},{16,24},{1,9},{9,17},{17,25},{2,10},{10,18},{18,26},{... | collective-permute-start | bytes 442376
  728.9 16.2 %all-to-all-start.4 = ((bf16[4,17,2048]{2,1,0:T(8,128)(2,1)}), bf16[4,17,2048]{2,1,0:T(8,128)(2,1)S(1)}, u32[]{:S(2)}, u32[]{:S(2)}) async-start(bf16[4,17,2048]{2,1,0:T(8,128)(2,1)} %reshape.49), calls=%async_computation.4 | async-start | bytes 786432 | tf_op jit(solution)/shard_map/all_to_all | solution.py:105
  745.1 15.3 %all-to-all-start.6 = ((bf16[4,17,2048]{2,1,0:T(8,128)(2,1)}), bf16[4,17,2048]{2,1,0:T(8,128)(2,1)S(1)}, u32[]{:S(2)}, u32[]{:S(2)}) async-start(bf16[4,17,2048]{2,1,0:T(8,128)(2,1)} %reshape.53), calls=%async_computation.6 | async-start | bytes 786432 | tf_op jit(solution)/shard_map/all_to_all | solution.py:106
  750.2 11.2 %copy-start.1 = (bf16[28,2048]{1,0:T(8,128)(2,1)S(1)}, bf16[28,2048]{1,0:T(8,128)(2,1)}, u32[]{:S(2)}) copy-start(bf16[28,2048]{1,0:T(8,128)(2,1)} %param.7) | copy-start | bytes 344068
Sparse Core Ops, SparseCore 0:
  430.2 32.3 all-gather.2
  464.4 30.9 all-gather.4
  616.5 22.8 all-reduce.7
where the time goes:
time: 770 us; the launch traced here: 768 us
  waiting for transfers between devices  540 us (70%)
  matrix products  74 us (10%)
  blocking collectives  48.9 us (6%)
  local copies, waits for them, and re-layouts  46.5 us (6%)
  starting transfers between devices  43.2 us (6%)
  between operations  14.6 us (2%)
    all_to_all x1, waiting for transfers between devices, local(): lax.all_to_all(gate_saved, 'expert', split_axis=0, concat_axis=2, tiled=T...  171 us
    all_to_all x1, waiting for transfers between devices, local(): lax.all_to_all(up_saved, 'expert', split_axis=0, concat_axis=2, tiled=True)  171 us
    all_to_all x1, waiting for transfers between devices, local(): lax.all_to_all(down_saved, 'expert', split_axis=0, concat_axis=2, tiled=T...  98.5 us
    unnamed x1, blocking collectives  48.9 us
    unnamed x32, local copies, waits for them, and re-layouts  39.2 us
    all_gather x1, waiting for transfers between devices, local(): lax.all_gather(arrived[0], 'dp', axis=0, tiled=True)  34.1 us
    all_gather x1, waiting for transfers between devices, local(): lax.all_gather(arrived[1], 'dp', axis=0, tiled=True)  31.2 us
    dot_general x3, matrix products, contract_rows(): lax.dot_general(left_side, right_side, (((0,), (0,)), ((), ())), preferre...  29.1 us
  transfers between devices with their start and end apart: 12, of which 8 were waited for; matrix products, arithmetic and copies ran while one was open for 11% of the time, Pallas kernels for 0%

commit v1 on v0

v1 whole, which is shorter than its diff:
```python
import jax
import jax.numpy as jnp
from jax import lax
from jax.sharding import PartitionSpec as P

BLOCKS = ("dp", "expert")
F32 = jnp.float32
BF16 = jnp.bfloat16


def swiglu_pair(gate_sum, up_sum, back_sum):
    sigmoid_gate = jax.nn.sigmoid(gate_sum)
    silu_gate = gate_sum * sigmoid_gate
    hidden = (silu_gate * up_sum).astype(BF16)
    d_up = (back_sum * silu_gate).astype(BF16)
    d_gate = (back_sum * up_sum * sigmoid_gate * (1.0 + gate_sum * (1.0 - sigmoid_gate))).astype(BF16)
    return (hidden, d_gate, d_up)


def contract_rows(left_side, right_side):
    return lax.dot_general(
        left_side, right_side, (((0,), (0,)), ((), ())), preferred_element_type=F32
    )


def feature_sum(part):
    if lax.axis_size("tensor") == 2:
        other = lax.ppermute(part, "tensor", [(0, 1), (1, 0)])
        return part.astype(F32) + other.astype(F32)
    return lax.psum(part, "tensor").astype(F32)


def join_lanes(piece):
    count = lax.axis_size("tensor")
    if count == 2:
        other = lax.ppermute(piece, "tensor", [(0, 1), (1, 0)])
        first = lax.axis_index("tensor") == 0
        return jnp.concatenate(
            [jnp.where(first, piece, other), jnp.where(first, other, piece)], axis=-1
        )
    return lax.all_gather(piece, "tensor", axis=piece.ndim - 1, tiled=True)


def local(tokens, route_ids, route_gates, d_out, gate_saved, up_saved, down_saved):
    experts = lax.axis_size("expert")
    blocks = lax.axis_size("dp") * experts
    tok_count, width = tokens.shape
    capacity = 5 * tok_count // 8
    rows = blocks * capacity
    hidden_width = gate_saved.shape[2]
    block = lax.axis_index("dp") * experts + lax.axis_index("expert")

    flat_ids = route_ids.reshape(-1)
    order = jnp.arange(2 * tok_count, dtype=jnp.int32)
    earlier = (flat_ids[None, :] == flat_ids[:, None]) & (order[None, :] < order[:, None])
    slot = jnp.sum(earlier.astype(jnp.int32), axis=1).reshape(tok_count, 2)
    target = route_ids * rows + block * capacity + slot
    routes = jnp.concatenate([target.astype(F32), route_gates], axis=1)
    routes = lax.all_gather(routes, BLOCKS, axis=0, tiled=False).reshape(-1, 4)
    all_tokens = lax.all_gather(tokens, BLOCKS, axis=0, tiled=False).reshape(-1, width)
    all_d_out = lax.all_gather(d_out, BLOCKS, axis=0, tiled=False).reshape(-1, width)

    targets = routes[:, :2].astype(jnp.int32).T
    gates = routes[:, 2:].T
    places = jnp.arange(experts * rows, dtype=jnp.int32)[:, None]
    first, second = places == targets[0][None], places == targets[1][None]
    placer = (first | second).astype(BF16)
    row_gates = jnp.sum(
        jnp.where(first, gates[0][None], 0.0) + jnp.where(second, gates[1][None], 0.0),
        axis=1, keepdims=True,
    )
    rows_x = jnp.dot(placer, all_tokens, preferred_element_type=F32)
    rows_x = rows_x.astype(BF16).reshape(experts, rows, width)
    rows_dy = jnp.dot(placer, all_d_out, preferred_element_type=F32) * row_gates
    rows_dy = rows_dy.astype(BF16).reshape(experts, rows, width)

    def forward(left, right):
        return jnp.einsum("erd,edf->erf", left, right, preferred_element_type=F32).astype(BF16)

    def backward(left, right):
        return jnp.einsum("erf,edf->erd", left, right, preferred_element_type=F32)

    gate_sum = feature_sum(forward(rows_x, gate_saved))
    up_sum = feature_sum(forward(rows_x, up_saved))
    back_sum = feature_sum(forward(rows_dy, down_saved))
    hidden, d_gate, d_up = swiglu_pair(gate_sum, up_sum, back_sum)

    share = hidden_width // lax.axis_size("tensor")
    start = lax.axis_index("tensor") * share

    def to_owner(array):
        piece = lax.dynamic_slice_in_dim(array, start, share, axis=2)
        piece = lax.all_to_all(piece, "expert", split_axis=0, concat_axis=0, tiled=True)
        piece = join_lanes(piece)
        return piece.transpose(1, 0, 2).reshape(rows, experts * hidden_width)

    own_hidden, own_d_gate, own_d_up = to_owner(hidden), to_owner(d_gate), to_owner(d_up)

    def to_tokens(slot_rows):
        sums = contract_rows(placer, slot_rows.reshape(experts * rows, width).astype(BF16))
        sums = sums.astype(BF16).reshape(blocks, tok_count, width)
        return lax.psum_scatter(sums, BLOCKS, scatter_dimension=0, tiled=False)

    out = to_tokens(backward(hidden, down_saved) * row_gates.reshape(experts, rows, 1))
    d_tokens = to_tokens(backward(d_gate, gate_saved) + backward(d_up, up_saved))

    mine = lax.axis_index("expert")
    own_x = lax.dynamic_index_in_dim(rows_x, mine, 0, keepdims=False)
    own_dy = lax.dynamic_index_in_dim(rows_dy, mine, 0, keepdims=False)
    grad_gate = contract_rows(own_x, own_d_gate).astype(BF16)[None]
    grad_up = contract_rows(own_x, own_d_up).astype(BF16)[None]
    grad_down = contract_rows(own_dy, own_hidden).astype(BF16)[None]
    return (out, d_tokens, grad_gate, grad_up, grad_down)


def solution(mesh):
    in_specs = (
        P(BLOCKS, "tensor"),
        P(BLOCKS, None),
        P(BLOCKS, None),
        P(BLOCKS, "tensor"),
        P(None, "tensor", BLOCKS),
        P(None, "tensor", BLOCKS),
        P(None, "tensor", BLOCKS),
    )
    out_specs = (
        P(BLOCKS, "tensor"),
        P(BLOCKS, "tensor"),
        P("expert", "tensor", "dp"),
        P("expert", "tensor", "dp"),
        P("expert", "tensor", "dp"),
    )
    return jax.shard_map(local, mesh=mesh, in_specs=in_specs, out_specs=out_specs, check_vma=False)
```

time: 770 us -> 359 us (0.47)
  waiting for transfers between devices: 540 us -> 182 us
  local copies, waits for them, and re-layouts: 46.5 us -> 15.9 us
  starting transfers between devices: 43.2 us -> 14.5 us
    all_to_all x7 -> x3, waiting for transfers between devices: 452 us -> 45.9 us  [to_owner(): lax.all_to_all(piece, 'expert', split_axis=0, concat_axis=0, tiled=True)]
    reduce_scatter x0 -> x2, waiting for transfers between devices: none -> 63.3 us  [to_tokens(): return lax.psum_scatter(sums, BLOCKS, scatter_dimension=0, tiled=False)]
    unnamed x1 -> x0, blocking collectives: 48.9 us -> none
    all_gather x0 -> x1, blocking collectives: none -> 42.8 us  [local(): routes = lax.all_gather(routes, BLOCKS, axis=0, tiled=False).reshape(-1, 4)]
    unnamed x32 -> x20, local copies, waits for them, and re-layouts: 39.2 us -> 7.29 us
    all_to_all x7 -> x3, starting transfers between devices: 36.4 us -> 13.2 us  [to_owner(): lax.all_to_all(piece, 'expert', split_axis=0, concat_axis=0, tiled=True)]
    psum x1 -> x0, waiting for transfers between devices: 21.2 us -> none  [local(): lax.psum(up_part.astype(jnp.bfloat16), 'tensor').astype(jnp.float32)]
    dot_general x10 -> x8, matrix products: 44.9 us -> 49.6 us  [the longest x3 25.9 us: backward(): return jnp.einsum('erf,edf->erd', left, right, preferred_element_type=F32)]
  transfers between devices with their start and end apart: 12 -> 13, of which waited for: 8 -> 8; matrix products, arithmetic and copies ran while one was open for 11% -> 24% of each run, Pallas kernels for 0% -> 0%
where the time goes in v1:
time: 359 us; the launch traced here: 358 us
  waiting for transfers between devices  182 us (51%)
  matrix products  80.3 us (22%)
  blocking collectives  42.8 us (12%)
  local copies, waits for them, and re-layouts  15.9 us (4%)
  starting transfers between devices  14.5 us (4%)
  between operations  14.1 us (4%)
  other arithmetic  8.33 us (2%)
    reduce_scatter x2, waiting for transfers between devices, to_tokens(): return lax.psum_scatter(sums, BLOCKS, scatter_dimension=0, tiled=False)  63.3 us
    all_gather x1, waiting for transfers between devices, local(): lax.all_gather(tokens, BLOCKS, axis=0, tiled=False).reshape(-1, width)  49.5 us
    all_to_all x3, waiting for transfers between devices, to_owner(): lax.all_to_all(piece, 'expert', split_axis=0, concat_axis=0, tiled=True)  45.9 us
    all_gather x1, blocking collectives, local(): routes = lax.all_gather(routes, BLOCKS, axis=0, tiled=False).reshape(-1, 4)  42.8 us
    dot_general x5, matrix products, contract_rows(): lax.dot_general(left_side, right_side, (((0,), (0,)), ((), ())), preferre...  30.7 us
    dot_general x3, matrix products, backward(): return jnp.einsum('erf,edf->erd', left, right, preferred_element_type=F32)  25.9 us
    all_gather x1, waiting for transfers between devices, local(): lax.all_gather(d_out, BLOCKS, axis=0, tiled=False).reshape(-1, width)  19.5 us
    dot_general x3, matrix products, forward(): jnp.einsum('erd,edf->erf', left, right, preferred_element_type=F32)  18.5 us
  transfers between devices with their start and end apart: 13, of which 8 were waited for; matrix products, arithmetic and copies ran while one was open for 24% of the time, Pallas kernels for 0%

profile of v1, /device:TPU:0, one launch (start us, length us, event | category | flops | bytes accessed | tf_op | source)
XLA Modules:
  0.0 358.4 jit_solution(10483835793634418669)
XLA Ops:
  7.2 0.0 all-gather.11.cloned.1.call-start
  7.2 0.7 all-gather.11.cloned.1.call-update
  7.9 0.0 all-gather.9.cloned.1.call-start
  7.9 0.7 all-gather.9.cloned.1.call-update
  8.6 0.0 reduce-scatter.3.cloned.1.call-start
  8.7 0.8 copy.46
  9.5 0.1 eq.51
  9.6 0.2 convert_reduce_fusion
  9.8 0.1 reshape.51
  9.9 0.1 copy.47
  10.0 0.7 add_convert_fusion.1
  10.6 0.7 maximum_bitcast_fusion.3
  11.3 42.8 %all-gather.3 = f32[16,28,4]{1,2,0:T(4,128)S(1)} all-gather(f32[1,28,4]{1,2,0:T(4,128)S(1)} %maximum_bitcast_fusion.3), channel_id=2, replica_groups=mesh['dp'=4,'expert'=4,'tensor'=2] {'dp','expert'}, dimensions={0}, use_global_device_ids=true | all-gather | bytes 7616 | tf_op jit(solution)/shard_map/all_gather | solution.py:59
  54.2 0.1 reshape.69
  54.3 0.6 add_reduce_fusion
  54.9 19.5 %all-gather.11.cloned.1.call-done = bf16[16,28,2048]{2,1,0:T(8,128)(2,1)} async-done(((bf16[1,28,2048]{2,1,0:T(8,128)(2,1)}), bf16[16,28,2048]{2,1,0:T(8,128)(2,1)}) %all-gather.11.cloned.1.call-update) | async-done | bytes 1835024 | tf_op jit(solution)/shard_map/all_gather | solution.py:61
  74.3 2.5 reshape.73
  76.8 2.6 fusion
  79.5 7.5 %convolution_convert_fusion.3 = bf16[4,272,512]{2,1,0:T(8,128)(2,1)S(1)} fusion(bf16[4,272,2048]{2,1,0:T(8,128)(2,1)S(1)} %bitcast.87, bf16[4,2048,512]{2,1,0:T(8,128)(2,1)} %param.13), kind=kOutput, calls=%fused_computation.22 | convolution fusion | flops 2282258432 | bytes 13959168 | tf_op jit(solution)/shard_map/erd,edf->erf/dot_general | solution.py:78
  87.0 0.1 collective-permute-start.2
  87.1 49.5 %all-gather.9.cloned.1.call-done = bf16[16,28,2048]{2,1,0:T(8,128)(2,1)} async-done(((bf16[1,28,2048]{2,1,0:T(8,128)(2,1)}), bf16[16,28,2048]{2,1,0:T(8,128)(2,1)}) %all-gather.9.cloned.1.call-update) | async-done | bytes 1835024 | tf_op jit(solution)/shard_map/all_gather | solution.py:60
  136.6 2.6 reshape.71
  139.2 2.6 convolution_convert_fusion
  141.9 7.5 %convolution_convert_fusion.5 = bf16[4,272,512]{2,1,0:T(8,128)(2,1)S(1)} fusion(bf16[4,272,2048]{2,1,0:T(8,128)(2,1)S(1)} %bitcast.89, bf16[4,2048,512]{2,1,0:T(8,128)(2,1)} %param.11), kind=kOutput, calls=%fused_computation.24 | convolution fusion | flops 2282258432 | bytes 13959168 | tf_op jit(solution)/shard_map/erd,edf->erf/dot_general | solution.py:78
  149.4 0.1 collective-permute-start
  149.5 3.5 convolution_convert_fusion.4
  153.0 0.5 collective-permute-start.1
  153.5 0.1 mul.60
  153.6 2.6 collective-permute-done.1
  156.2 4.6 %multiply_convert_fusion.1 = (bf16[4,272,512]{2,1,0:T(8,128)(2,1)S(1)}, bf16[4,272,512]{2,1,0:T(8,128)(2,1)S(1)}, bf16[4,272,512]{2,1,0:T(8,128)(2,1)S(1)}) fusion(bf16[4,272,512]{2,1,0:T(8,128)(2,1)} %collective-permute-done.2, bf16[4,272,512]{2,1,0:T(8,128)(2,1)} %copy-done, bf16[4,272,512]{2,1,0:T(8,128)(2,1)} %collective-permute-done, ...), kind=kLoop, calls=%fused_computation.10 | loop fusion | flops 13369344 | bytes 10027008 | tf_op jit(solution)/shard_map/convert_element_type | solution.py:15
  160.8 5.9 %multiply_convert_fusion = bf16[4,272,2048]{2,1,0:T(8,128)(2,1)S(1)} fusion(f32[4,272]{1,0:T(4,128)S(1)} %mul.60, bf16[4,272,512]{2,1,0:T(8,128)(2,1)S(1)} %get-tuple-element.7, bf16[4,2048,512]{2,1,0:T(8,128)(2,1)} %param.13), kind=kOutput, calls=%fused_computation.2 | convolution fusion | flops 2286157824 | bytes 13963520 | tf_op jit(solution)/shard_map/erf,edf->erd/dot_general | solution.py:81
  166.7 4.1 %convolution_convert_fusion.2 = bf16[448,2048]{1,0:T(8,128)(2,1)} fusion(bf16[1088,2048]{1,0:T(8,128)(2,1)S(1)} %bitcast.95, s32[448]{0:T(512)S(1)} %bitcast.81, s32[448]{0:T(512)S(1)} %bitcast.76), kind=kOutput, calls=%fused_computation.9 | convolution fusion | flops 1998868480 | bytes 6295040 | tf_op jit(solution)/shard_map/dot_general | solution.py:21
  170.8 3.5 reshape.55
  174.4 0.8 constant_dynamic-slice_fusion.2
  175.2 4.2 %all-to-all-start = ((bf16[4,272,256]{2,1,0:T(8,128)(2,1)}), bf16[4,272,256]{2,1,0:T(8,128)(2,1)}, u32[]{:S(2)}, u32[]{:S(2)}) async-start(bf16[4,272,256]{2,1,0:T(8,128)(2,1)} %constant_dynamic-slice_fusion.2), calls=%async_computation.2 | async-start | bytes 1114112 | tf_op jit(solution)/shard_map/all_to_all | solution.py:93
  179.4 0.9 constant_dynamic-slice_fusion
  180.3 0.8 constant_dynamic-slice_fusion.1
  181.1 9.4 %fusion.20 = f32[4,272,2048]{2,1,0:T(8,128)} fusion(bf16[4,272,512]{2,1,0:T(8,128)(2,1)S(1)} %get-tuple-element.6, bf16[4,2048,512]{2,1,0:T(8,128)(2,1)} %param.11), kind=kOutput, calls=%fused_computation.56 | convolution fusion | flops 2281701376 | bytes 18415616 | tf_op jit(solution)/shard_map/erf,edf->erd/dot_general | solution.py:81
  190.5 17.8 %all-to-all-done = bf16[4,272,256]{2,1,0:T(8,128)(2,1)} async-done(((bf16[4,272,256]{2,1,0:T(8,128)(2,1)}), bf16[4,272,256]{2,1,0:T(8,128)(2,1)}, u32[]{:S(2)}, u32[]{:S(2)}) %all-to-all-start) | async-done | bytes 557088 | tf_op jit(solution)/shard_map/all_to_all | solution.py:93
  208.2 3.5 all-to-all-start.1
  211.7 10.6 %add_convert_fusion = bf16[4,272,2048]{2,1,0:T(8,128)(2,1)} fusion(f32[4,272,2048]{2,1,0:T(8,128)} %fusion.20, bf16[4,272,512]{2,1,0:T(8,128)(2,1)S(1)} %get-tuple-element.5, bf16[4,2048,512]{2,1,0:T(8,128)(2,1)} %param.12), kind=kOutput, calls=%fused_computation.1 | convolution fusion | flops 2286157824 | bytes 22872064 | tf_op jit(solution)/shard_map/erf,edf->erd/dot_general | solution.py:81
  222.3 13.6 %all-to-all-done.1 = bf16[4,272,256]{2,1,0:T(8,128)(2,1)S(1)} async-done(((bf16[4,272,256]{2,1,0:T(8,128)(2,1)}), bf16[4,272,256]{2,1,0:T(8,128)(2,1)S(1)}, u32[]{:S(2)}, u32[]{:S(2)}) %all-to-all-start.1) | async-done | bytes 557088 | tf_op jit(solution)/shard_map/all_to_all | solution.py:93
  235.9 5.6 %all-to-all-start.2 = ((bf16[4,272,256]{2,1,0:T(8,128)(2,1)}), bf16[4,272,256]{2,1,0:T(8,128)(2,1)S(1)}, u32[]{:S(2)}, u32[]{:S(2)}) async-start(bf16[4,272,256]{2,1,0:T(8,128)(2,1)} %constant_dynamic-slice_fusion), calls=%async_computation.4 | async-start | bytes 1114112 | tf_op jit(solution)/shard_map/all_to_all | solution.py:93
  241.5 4.9 %convolution_convert_fusion.1 = bf16[448,2048]{1,0:T(8,128)(2,1)S(1)} fusion(bf16[1088,2048]{1,0:T(8,128)(2,1)} %bitcast.67, s32[448]{0:T(512)S(1)} %bitcast.82, s32[448]{0:T(512)S(1)} %bitcast.77), kind=kOutput, calls=%fused_computation.8 | convolution fusion | flops 1998868480 | bytes 6295040 | tf_op jit(solution)/shard_map/dot_general | solution.py:21
  246.4 1.8 reshape.58
  248.3 0.1 collective-permute-start.3
  248.3 0.5 collective-permute-start.4
  248.8 14.5 %all-to-all-done.2 = bf16[4,272,256]{2,1,0:T(8,128)(2,1)S(1)} async-done(((bf16[4,272,256]{2,1,0:T(8,128)(2,1)}), bf16[4,272,256]{2,1,0:T(8,128)(2,1)S(1)}, u32[]{:S(2)}, u32[]{:S(2)}) %all-to-all-start.2) | async-done | bytes 557088 | tf_op jit(solution)/shard_map/all_to_all | solution.py:93
  263.4 1.1 broadcast_select_fusion.5
  264.5 0.1 maximum_bitcast_fusion
  264.6 0.1 copy.52
  264.8 0.1 broadcast_select_fusion.3
  264.8 0.1 maximum_bitcast_fusion.1
  265.0 0.1 copy.53
  265.1 0.2 collective-permute-done.5
  265.3 0.1 broadcast_select_fusion.1
  265.4 0.1 maximum_bitcast_fusion.2
  265.5 0.1 copy.54
  265.6 1.2 slice-done.2
  266.8 0.1 slice-done.3
  266.9 6.8 %convert_bitcast_fusion.2 = bf16[1,2048,2048]{2,1,0:T(8,128)(2,1)} fusion(bf16[272,2048]{1,0:T(8,128)(2,1)S(1)} %bitcast.68, bf16[4,272,2048]{2,1,0:T(8,128)(2,1)S(1)} %bitcast.93, s32[]{:T(128)S(6)} %select_n.47), kind=kOutput, calls=%fused_computation.5 | convolution fusion | flops 2285895680 | bytes 10616836 | tf_op jit(solution)/shard_map/dot_general | solution.py:21
  273.7 6.8 %convert_bitcast_fusion.1 = bf16[1,2048,2048]{2,1,0:T(8,128)(2,1)} fusion(bf16[272,2048]{1,0:T(8,128)(2,1)S(1)} %bitcast.69, bf16[4,272,2048]{2,1,0:T(8,128)(2,1)S(1)} %bitcast.94, s32[]{:T(128)S(6)} %select_n.47), kind=kOutput, calls=%fused_computation.4 | convolution fusion | flops 2285895680 | bytes 10616836 | tf_op jit(solution)/shard_map/dot_general | solution.py:21
  280.5 8.0 %convert_bitcast_fusion = bf16[1,2048,2048]{2,1,0:T(8,128)(2,1)} fusion(bf16[272,2048]{1,0:T(8,128)(2,1)S(1)} %bitcast.70, bf16[4,272,2048]{2,1,0:T(8,128)(2,1)} %bitcast.88, s32[]{:T(128)S(6)} %select_n.47), kind=kOutput, calls=%fused_computation.3 | convolution fusion | flops 2285895680 | bytes 10616836 | tf_op jit(solution)/shard_map/dot_general | solution.py:21
  288.6 63.3 %reduce-scatter.5.cloned.1.call-done = bf16[1,28,2048]{2,1,0:T(8,128)(2,1)} async-done(((bf16[16,28,2048]{2,1,0:T(8,128)(2,1)}), bf16[1,28,2048]{2,1,0:T(8,128)(2,1)}) %reduce-scatter.5.cloned.1.call-update) | async-done | bytes 114704 | tf_op jit(solution)/shard_map/reduce_scatter | solution.py:102
  (29 shorter events, 0.1 us)
Async XLA Ops:
  7.2 67.2 %all-gather.11.cloned.1.call-start = ((), (), s32[]{:S(2)}) async-start(), calls=%async_computation.8 | async-start | bytes 2228224 | tf_op jit(solution)/shard_map/all_gather | solution.py:61
  7.9 128.7 %all-gather.9.cloned.1.call-start = ((), (), s32[]{:S(2)}) async-start(), calls=%async_computation.7 | async-start | bytes 2228224 | tf_op jit(solution)/shard_map/all_gather | solution.py:60
  8.6 279.9 %reduce-scatter.3.cloned.1.call-start = ((), (), s32[]{:S(2)}) async-start(), calls=%async_computation.5 | async-start | bytes 2228224 | tf_op jit(solution)/shard_map/reduce_scatter | solution.py:102
  79.4 7.5 %copy-start.2 = (bf16[1088,2048]{1,0:T(8,128)(2,1)}, bf16[1088,2048]{1,0:T(8,128)(2,1)S(1)}, u32[]{:S(2)}) copy-start(bf16[1088,2048]{1,0:T(8,128)(2,1)S(1)} %fusion) | copy-start | bytes 13369348
  87.0 54.9 %copy-start = (bf16[4,272,512]{2,1,0:T(8,128)(2,1)}, bf16[4,272,512]{2,1,0:T(8,128)(2,1)S(1)}, u32[]{:S(2)}) copy-start(bf16[4,272,512]{2,1,0:T(8,128)(2,1)S(1)} %convolution_convert_fusion.3) | copy-start | bytes 3342340
  87.0 66.5 %collective-permute-start.2 = (bf16[4,272,512]{2,1,0:T(8,128)(2,1)S(1)}, bf16[4,272,512]{2,1,0:T(8,128)(2,1)}, u32[]{:S(2)}, u32[]{:S(2)}) collective-permute-start(bf16[4,272,512]{2,1,0:T(8,128)(2,1)S(1)} %convolution_convert_fusion.3), channel_id=1, source_target_pairs={{0,1},{1,0},{2,3},{3,2},{4,5},{5,4},{6,7},{7,6},{8,9},{9,8},{10,11... | collective-permute-start | bytes 3342344 | tf_op jit(solution)/shard_map/ppermute | solution.py:28
  139.2 10.3 %slice-start = ((s8[8388608]{0:T(1024)(128)(4,1)}), s8[4194304]{0:T(1024)(128)(4,1)S(1)}, s32[]{:S(2)}) async-start(s8[8388608]{0:T(1024)(128)(4,1)} %bitcast.65), calls=%async_computation.9 | async-start | bytes 8388608
  141.9 7.6 %copy-start.3 = (bf16[1088,2048]{1,0:T(8,128)(2,1)}, bf16[1088,2048]{1,0:T(8,128)(2,1)S(1)}, u32[]{:S(2)}) copy-start(bf16[1088,2048]{1,0:T(8,128)(2,1)S(1)} %convolution_convert_fusion) | copy-start | bytes 13369348
  141.9 7.6 %slice-start.1 = ((s8[8388608]{0:T(1024)(128)(4,1)}), s8[4194304]{0:T(1024)(128)(4,1)S(1)}, s32[]{:S(2)}) async-start(s8[8388608]{0:T(1024)(128)(4,1)} %bitcast.65), calls=%async_computation.10 | async-start | bytes 8388608
  149.4 3.6 %copy-start.1 = (bf16[4,272,512]{2,1,0:T(8,128)(2,1)}, bf16[4,272,512]{2,1,0:T(8,128)(2,1)S(1)}, u32[]{:S(2)}) copy-start(bf16[4,272,512]{2,1,0:T(8,128)(2,1)S(1)} %convolution_convert_fusion.5) | copy-start | bytes 3342340
  149.4 4.2 %collective-permute-start = (bf16[4,272,512]{2,1,0:T(8,128)(2,1)S(1)}, bf16[4,272,512]{2,1,0:T(8,128)(2,1)}, u32[]{:S(2)}, u32[]{:S(2)}) collective-permute-start(bf16[4,272,512]{2,1,0:T(8,128)(2,1)S(1)} %convolution_convert_fusion.5), channel_id=1, source_target_pairs={{0,1},{1,0},{2,3},{3,2},{4,5},{5,4},{6,7},{7,6},{8,9},{9,8},{10,11... | collective-permute-start | bytes 3342344 | tf_op jit(solution)/shard_map/ppermute | solution.py:28
  153.0 3.2 collective-permute-start.1
  175.2 33.0 %all-to-all-start = ((bf16[4,272,256]{2,1,0:T(8,128)(2,1)}), bf16[4,272,256]{2,1,0:T(8,128)(2,1)}, u32[]{:S(2)}, u32[]{:S(2)}) async-start(bf16[4,272,256]{2,1,0:T(8,128)(2,1)} %constant_dynamic-slice_fusion.2), calls=%async_computation.2 | async-start | bytes 1114112 | tf_op jit(solution)/shard_map/all_to_all | solution.py:93
  208.2 27.7 %all-to-all-start.1 = ((bf16[4,272,256]{2,1,0:T(8,128)(2,1)}), bf16[4,272,256]{2,1,0:T(8,128)(2,1)S(1)}, u32[]{:S(2)}, u32[]{:S(2)}) async-start(bf16[4,272,256]{2,1,0:T(8,128)(2,1)} %constant_dynamic-slice_fusion.1), calls=%async_computation.3 | async-start | bytes 1114112 | tf_op jit(solution)/shard_map/all_to_all | solution.py:93
  235.9 27.5 %all-to-all-start.2 = ((bf16[4,272,256]{2,1,0:T(8,128)(2,1)}), bf16[4,272,256]{2,1,0:T(8,128)(2,1)S(1)}, u32[]{:S(2)}, u32[]{:S(2)}) async-start(bf16[4,272,256]{2,1,0:T(8,128)(2,1)} %constant_dynamic-slice_fusion), calls=%async_computation.4 | async-start | bytes 1114112 | tf_op jit(solution)/shard_map/all_to_all | solution.py:93
  241.5 110.4 %reduce-scatter.5.cloned.1.call-start = ((), (), s32[]{:S(2)}) async-start(), calls=%async_computation.6 | async-start | bytes 2228224 | tf_op jit(solution)/shard_map/reduce_scatter | solution.py:102
  248.3 15.1 %collective-permute-start.3 = (bf16[4,272,256]{2,1,0:T(8,128)(2,1)}, bf16[4,272,256]{2,1,0:T(8,128)(2,1)S(1)}, u32[]{:S(2)}, u32[]{:S(2)}) collective-permute-start(bf16[4,272,256]{2,1,0:T(8,128)(2,1)} %all-to-all-done), channel_id=1, source_target_pairs={{0,1},{1,0},{2,3},{3,2},{4,5},{5,4},{6,7},{7,6},{8,9},{9,8},{10,11... | collective-permute-start | bytes 1671176 | tf_op jit(solution)/shard_map/ppermute | solution.py:36
  248.3 16.4 %collective-permute-start.4 = (bf16[4,272,256]{2,1,0:T(8,128)(2,1)S(1)}, bf16[4,272,256]{2,1,0:T(8,128)(2,1)S(1)}, u32[]{:S(2)}, u32[]{:S(2)}) collective-permute-start(bf16[4,272,256]{2,1,0:T(8,128)(2,1)S(1)} %all-to-all-done.1), channel_id=1, source_target_pairs={{0,1},{1,0},{2,3},{3,2},{4,5},{5,4},{6,7},{7,6},{8,9},{9,8},{10,11... | collective-permute-start | bytes 1671176 | tf_op jit(solution)/shard_map/ppermute | solution.py:36
  263.4 2.0 collective-permute-start.5
  264.6 2.2 slice-start.2
  264.9 2.0 slice-start.3
Sparse Core Ops, SparseCore 0:
  10.8 63.4 all-gather.10
  77.1 59.3 all-gather.8
  174.5 91.3 reduce-scatter.2
  268.6 83.2 reduce-scatter.4

commit v2 on v1

--- a/solution.py
+++ b/solution.py
@@ -41,6 +41,16 @@
     return lax.all_gather(piece, "tensor", axis=piece.ndim - 1, tiled=True)
 
 
+def spread(block, axes):
+    copies = jnp.broadcast_to(block[None], (lax.axis_size(axes),) + block.shape)
+    return lax.all_to_all(copies, axes, split_axis=0, concat_axis=0, tiled=True)
+
+
+def collect(sums, axis):
+    parts = lax.all_to_all(sums, axis, split_axis=0, concat_axis=0, tiled=True)
+    return jnp.sum(parts.astype(F32), axis=0).astype(BF16)
+
+
 def local(tokens, route_ids, route_gates, d_out, gate_saved, up_saved, down_saved):
     experts = lax.axis_size("expert")
     blocks = lax.axis_size("dp") * experts
@@ -56,9 +66,17 @@
     slot = jnp.sum(earlier.astype(jnp.int32), axis=1).reshape(tok_count, 2)
     target = route_ids * rows + block * capacity + slot
     routes = jnp.concatenate([target.astype(F32), route_gates], axis=1)
-    routes = lax.all_gather(routes, BLOCKS, axis=0, tiled=False).reshape(-1, 4)
-    all_tokens = lax.all_gather(tokens, BLOCKS, axis=0, tiled=False).reshape(-1, width)
-    all_d_out = lax.all_gather(d_out, BLOCKS, axis=0, tiled=False).reshape(-1, width)
+    padding = -tok_count % 16
+    padded = tok_count + padding
+    routes = jnp.pad(routes, ((0, padding), (0, 0)), constant_values=-1.0)
+    routes = spread(routes, BLOCKS).reshape(-1, 4)
+
+    def gather(own):
+        own = jnp.pad(own, ((0, padding), (0, 0)))
+        return spread(spread(own, "expert"), "dp").reshape(-1, width)
+
+    all_tokens = gather(tokens)
+    all_d_out = gather(d_out)
 
     targets = routes[:, :2].astype(jnp.int32).T
     gates = routes[:, 2:].T
@@ -98,8 +116,8 @@
 
     def to_tokens(slot_rows):
         sums = contract_rows(placer, slot_rows.reshape(experts * rows, width).astype(BF16))
-        sums = sums.astype(BF16).reshape(blocks, tok_count, width)
-        return lax.psum_scatter(sums, BLOCKS, scatter_dimension=0, tiled=False)
+        sums = sums.astype(BF16).reshape(-1, experts, padded, width)
+        return collect(collect(sums, "dp"), "expert")[:tok_count]
 
     out = to_tokens(backward(hidden, down_saved) * row_gates.reshape(experts, rows, 1))
     d_tokens = to_tokens(backward(d_gate, gate_saved) + backward(d_up, up_saved))

time: 359 us -> 293 us (0.82)
  waiting for transfers between devices: 182 us -> 102 us
  starting transfers between devices: 14.5 us -> 47.2 us
  blocking collectives: 42.8 us -> 16.2 us
  between operations: 14.1 us -> 1.04 us
  other arithmetic: 8.33 us -> 19.1 us
  matrix products: 80.3 us -> 90.3 us
    all_to_all x0 -> x8, waiting for transfers between devices: none -> 78.2 us  [the longest x4 55.8 us: spread(): return lax.all_to_all(copies, axes, split_axis=0, concat_axis=0, tiled=True)]
    all_gather x2 -> x0, waiting for transfers between devices: 68.9 us -> none  [the longest x1 49.5 us: local(): lax.all_gather(tokens, BLOCKS, axis=0, tiled=False).reshape(-1, width)]
    reduce_scatter x2 -> x0, waiting for transfers between devices: 63.3 us -> none  [to_tokens(): return lax.psum_scatter(sums, BLOCKS, scatter_dimension=0, tiled=False)]
    all_gather x1 -> x0, blocking collectives: 42.8 us -> none  [local(): routes = lax.all_gather(routes, BLOCKS, axis=0, tiled=False).reshape(-1, 4)]
    all_to_all x0 -> x8, starting transfers between devices: none -> 35.5 us  [the longest x4 19.9 us: spread(): return lax.all_to_all(copies, axes, split_axis=0, concat_axis=0, tiled=True)]
    all_to_all x3, waiting for transfers between devices: 45.9 us -> 19.9 us  [to_owner(): lax.all_to_all(piece, 'expert', split_axis=0, concat_axis=0, tiled=True)]
    all_to_all x0 -> x1, blocking collectives: none -> 16.2 us  [spread(): return lax.all_to_all(copies, axes, split_axis=0, concat_axis=0, tiled=True)]
    reduce_sum x0 -> x4, other arithmetic: none -> 6.78 us  [collect(): return jnp.sum(parts.astype(F32), axis=0).astype(BF16)]
  transfers between devices with their start and end apart: 13 -> 17, of which waited for: 8 -> 12; matrix products, arithmetic and copies ran while one was open for 24% -> 36% of each run, Pallas kernels for 0% -> 0%
where the time goes in v2:
time: 293 us; the launch traced here: 292 us
  waiting for transfers between devices  102 us (35%)
  matrix products  90.3 us (31%)
  starting transfers between devices  47.2 us (16%)
  other arithmetic  19.1 us (7%)
  local copies, waits for them, and re-layouts  16.3 us (6%)
  blocking collectives  16.2 us (6%)
    all_to_all x4, waiting for transfers between devices, spread(): return lax.all_to_all(copies, axes, split_axis=0, concat_axis=0, tiled=True)  55.8 us
    dot_general x5, matrix products, contract_rows(): lax.dot_general(left_side, right_side, (((0,), (0,)), ((), ())), preferre...  37 us
    dot_general x3, matrix products, backward(): return jnp.einsum('erf,edf->erd', left, right, preferred_element_type=F32)  28.2 us
    all_to_all x4, waiting for transfers between devices, collect(): parts = lax.all_to_all(sums, axis, split_axis=0, concat_axis=0, tiled=True)  22.4 us
    all_to_all x3, waiting for transfers between devices, to_owner(): lax.all_to_all(piece, 'expert', split_axis=0, concat_axis=0, tiled=True)  19.9 us
    all_to_all x4, starting transfers between devices, spread(): return lax.all_to_all(copies, axes, split_axis=0, concat_axis=0, tiled=True)  19.9 us
    dot_general x3, matrix products, forward(): jnp.einsum('erd,edf->erf', left, right, preferred_element_type=F32)  18.4 us
    all_to_all x1, blocking collectives, spread(): return lax.all_to_all(copies, axes, split_axis=0, concat_axis=0, tiled=True)  16.2 us
  transfers between devices with their start and end apart: 17, of which 12 were waited for; matrix products, arithmetic and copies ran while one was open for 36% of the time, Pallas kernels for 0%

profile of v2, /device:TPU:0, one launch (start us, length us, event | category | flops | bytes accessed | tf_op | source)
XLA Modules:
  0.0 291.8 jit_solution(13474240572671497839)
XLA Ops:
  0.6 0.8 copy.52
  1.9 0.7 add_convert_fusion.1
  2.6 0.7 select_maximum_fusion
  3.3 0.7 reshape.67
  4.0 8.3 %all-to-all-start = ((f32[16,1,128]{2,1,0:T(1,128)}), f32[16,1,128]{2,1,0:T(1,128)S(1)}, u32[]{:S(2)}, u32[]{:S(2)}) async-start(f32[16,1,128]{2,1,0:T(1,128)} %reshape.67), calls=%async_computation | async-start | bytes 16384 | tf_op jit(solution)/shard_map/all_to_all | solution.py:46
  12.3 0.9 pad.13
  13.3 6.3 %all-to-all-done = f32[16,1,128]{2,1,0:T(1,128)S(1)} async-done(((f32[16,1,128]{2,1,0:T(1,128)}), f32[16,1,128]{2,1,0:T(1,128)S(1)}, u32[]{:S(2)}, u32[]{:S(2)}) %all-to-all-start) | async-done | bytes 8224 | tf_op jit(solution)/shard_map/all_to_all | solution.py:46
  19.5 0.8 broadcast_in_dim.73
  20.4 3.5 %all-to-all-start.5 = ((bf16[4,32,2048]{2,1,0:T(8,128)(2,1)}), bf16[4,32,2048]{2,1,0:T(8,128)(2,1)S(1)}, u32[]{:S(2)}, u32[]{:S(2)}) async-start(bf16[4,32,2048]{2,1,0:T(8,128)(2,1)} %broadcast_in_dim.73), calls=%async_computation.5 | async-start | bytes 1048576 | tf_op jit(solution)/shard_map/all_to_all | solution.py:46
  23.9 13.3 %all-to-all-done.5 = bf16[4,32,2048]{2,1,0:T(8,128)(2,1)S(1)} async-done(((bf16[4,32,2048]{2,1,0:T(8,128)(2,1)}), bf16[4,32,2048]{2,1,0:T(8,128)(2,1)S(1)}, u32[]{:S(2)}, u32[]{:S(2)}) %all-to-all-start.5) | async-done | bytes 524320 | tf_op jit(solution)/shard_map/all_to_all | solution.py:46
  37.2 16.2 %all_to_all.60 = bf16[4,32,2048]{2,1,0:T(8,128)(2,1)S(1)} all-to-all(bf16[4,32,2048]{2,1,0:T(8,128)(2,1)S(1)} %broadcast_in_dim.66), channel_id=1, replica_groups=mesh['dp'=4,'expert'=4,'tensor'=2] {'expert'}, dimensions={0} | all-to-all | bytes 1048576 | tf_op jit(solution)/shard_map/all_to_all | solution.py:46
  53.4 1.6 broadcast_in_dim.74
  55.0 3.6 %all-to-all-start.6 = ((bf16[4,4,32,2048]{3,2,1,0:T(8,128)(2,1)}), bf16[4,4,32,2048]{3,2,1,0:T(8,128)(2,1)S(1)}, u32[]{:S(2)}, u32[]{:S(2)}) async-start(bf16[4,4,32,2048]{3,2,1,0:T(8,128)(2,1)} %broadcast_in_dim.74), calls=%async_computation.6 | async-start | bytes 4194304 | tf_op jit(solution)/shard_map/all_to_all | solution.py:46
  58.6 0.5 broadcast.28
  59.2 0.7 reduce.4
  60.0 22.5 %all-to-all-done.6 = bf16[4,4,32,2048]{3,2,1,0:T(8,128)(2,1)S(1)} async-done(((bf16[4,4,32,2048]{3,2,1,0:T(8,128)(2,1)}), bf16[4,4,32,2048]{3,2,1,0:T(8,128)(2,1)S(1)}, u32[]{:S(2)}, u32[]{:S(2)}) %all-to-all-start.6) | async-done | bytes 2097184 | tf_op jit(solution)/shard_map/all_to_all | solution.py:46
  82.5 1.6 broadcast_in_dim.67
  84.1 4.5 %all-to-all-start.2 = ((bf16[4,4,32,2048]{3,2,1,0:T(8,128)(2,1)}), bf16[4,4,32,2048]{3,2,1,0:T(8,128)(2,1)}, u32[]{:S(2)}, u32[]{:S(2)}) async-start(bf16[4,4,32,2048]{3,2,1,0:T(8,128)(2,1)} %broadcast_in_dim.67), calls=%async_computation.2 | async-start | bytes 4194304 | tf_op jit(solution)/shard_map/all_to_all | solution.py:46
  88.6 0.5 add_reduce_fusion
  89.2 2.5 fusion
  91.7 7.4 %convolution_convert_fusion.3 = bf16[4,272,512]{2,1,0:T(8,128)(2,1)S(1)} fusion(bf16[4,272,2048]{2,1,0:T(8,128)(2,1)S(1)} %bitcast.92, bf16[4,2048,512]{2,1,0:T(8,128)(2,1)} %param.13), kind=kOutput, calls=%fused_computation.22 | convolution fusion | flops 2282258432 | bytes 13959168 | tf_op jit(solution)/shard_map/erd,edf->erf/dot_general | solution.py:96
  99.3 13.7 %all-to-all-done.2 = bf16[4,4,32,2048]{3,2,1,0:T(8,128)(2,1)} async-done(((bf16[4,4,32,2048]{3,2,1,0:T(8,128)(2,1)}), bf16[4,4,32,2048]{3,2,1,0:T(8,128)(2,1)}, u32[]{:S(2)}, u32[]{:S(2)}) %all-to-all-start.2) | async-done | bytes 2097184 | tf_op jit(solution)/shard_map/all_to_all | solution.py:46
  113.0 4.2 %convolution_convert_fusion = bf16[1088,2048]{1,0:T(8,128)(2,1)S(1)} fusion(bf16[512,2048]{1,0:T(8,128)(2,1)} %bitcast.3, s32[512]{0:T(512)S(1)} %bitcast.87, s32[512]{0:T(512)S(1)} %bitcast.82), kind=kOutput, calls=%fused_computation.7 | convolution fusion | flops 2285600768 | bytes 6557696 | tf_op jit(solution)/shard_map/dot_general | solution.py:90
  117.3 7.5 %convolution_convert_fusion.5 = bf16[4,272,512]{2,1,0:T(8,128)(2,1)S(1)} fusion(bf16[4,272,2048]{2,1,0:T(8,128)(2,1)S(1)} %bitcast.94, bf16[4,2048,512]{2,1,0:T(8,128)(2,1)} %param.11), kind=kOutput, calls=%fused_computation.24 | convolution fusion | flops 2282258432 | bytes 13959168 | tf_op jit(solution)/shard_map/erd,edf->erf/dot_general | solution.py:96
  124.9 3.5 %convolution_convert_fusion.4 = bf16[4,272,512]{2,1,0:T(8,128)(2,1)} fusion(bf16[4,272,2048]{2,1,0:T(8,128)(2,1)S(1)} %bitcast.95, bf16[4,2048,512]{2,1,0:T(8,128)(2,1)S(1)} %bitcast.69), kind=kOutput, calls=%fused_computation.23 | convolution fusion | flops 2282258432 | bytes 13959168 | tf_op jit(solution)/shard_map/erd,edf->erf/dot_general | solution.py:96
  128.8 1.0 copy-done.7
  129.8 1.7 collective-permute-done.1
  131.5 5.8 %multiply_convert_fusion.1 = (bf16[4,272,512]{2,1,0:T(8,128)(2,1)S(1)}, bf16[4,272,512]{2,1,0:T(8,128)(2,1)S(1)}, bf16[4,272,512]{2,1,0:T(8,128)(2,1)}) fusion(bf16[4,272,512]{2,1,0:T(8,128)(2,1)} %copy-done.7, bf16[4,272,512]{2,1,0:T(8,128)(2,1)} %copy-done.6, bf16[4,272,512]{2,1,0:T(8,128)(2,1)} %collective-permute-done, ...), kind=kLoop, calls=%fused_computation.10 | loop fusion | flops 13369344 | bytes 10027008 | tf_op jit(solution)/shard_map/convert_element_type | solution.py:15
  137.3 0.8 constant_dynamic-slice_fusion.2
  138.2 3.5 %all-to-all-start.9 = ((bf16[4,272,256]{2,1,0:T(8,128)(2,1)}), bf16[4,272,256]{2,1,0:T(8,128)(2,1)S(1)}, u32[]{:S(2)}, u32[]{:S(2)}) async-start(bf16[4,272,256]{2,1,0:T(8,128)(2,1)} %constant_dynamic-slice_fusion.2), calls=%async_computation.9 | async-start | bytes 1114112 | tf_op jit(solution)/shard_map/all_to_all | solution.py:111
  141.7 0.9 constant_dynamic-slice_fusion.1
  142.6 15.0 %all-to-all-done.9 = bf16[4,272,256]{2,1,0:T(8,128)(2,1)S(1)} async-done(((bf16[4,272,256]{2,1,0:T(8,128)(2,1)}), bf16[4,272,256]{2,1,0:T(8,128)(2,1)S(1)}, u32[]{:S(2)}, u32[]{:S(2)}) %all-to-all-start.9) | async-done | bytes 557088 | tf_op jit(solution)/shard_map/all_to_all | solution.py:111
  157.6 0.8 copy-done.5
  158.4 3.5 %all-to-all-start.10 = ((bf16[4,272,256]{2,1,0:T(8,128)(2,1)}), bf16[4,272,256]{2,1,0:T(8,128)(2,1)S(1)}, u32[]{:S(2)}, u32[]{:S(2)}) async-start(bf16[4,272,256]{2,1,0:T(8,128)(2,1)} %constant_dynamic-slice_fusion.1), calls=%async_computation.10 | async-start | bytes 1114112 | tf_op jit(solution)/shard_map/all_to_all | solution.py:111
  161.9 1.9 constant_dynamic-slice_fusion
  163.8 8.3 %multiply_convert_fusion = bf16[4,272,2048]{2,1,0:T(8,128)(2,1)} fusion(f32[4,272]{1,0:T(4,128)S(1)} %mul.60, bf16[4,272,512]{2,1,0:T(8,128)(2,1)} %get-tuple-element.7, bf16[4,2048,512]{2,1,0:T(8,128)(2,1)} %param.13), kind=kOutput, calls=%fused_computation.2 | convolution fusion | flops 2286157824 | bytes 13963520 | tf_op jit(solution)/shard_map/erf,edf->erd/dot_general | solution.py:99
  172.1 4.9 %all-to-all-done.10 = bf16[4,272,256]{2,1,0:T(8,128)(2,1)S(1)} async-done(((bf16[4,272,256]{2,1,0:T(8,128)(2,1)}), bf16[4,272,256]{2,1,0:T(8,128)(2,1)S(1)}, u32[]{:S(2)}, u32[]{:S(2)}) %all-to-all-start.10) | async-done | bytes 557088 | tf_op jit(solution)/shard_map/all_to_all | solution.py:111
  177.1 0.8 copy-done.3
  177.9 3.5 %all-to-all-start.11 = ((bf16[4,272,256]{2,1,0:T(8,128)(2,1)}), bf16[4,272,256]{2,1,0:T(8,128)(2,1)S(1)}, u32[]{:S(2)}, u32[]{:S(2)}) async-start(bf16[4,272,256]{2,1,0:T(8,128)(2,1)} %constant_dynamic-slice_fusion), calls=%async_computation.11 | async-start | bytes 1114112 | tf_op jit(solution)/shard_map/all_to_all | solution.py:111
  181.4 6.4 %convolution_convert_fusion.2 = bf16[512,2048]{1,0:T(8,128)(2,1)} fusion(bf16[1088,2048]{1,0:T(8,128)(2,1)} %bitcast.98, s32[512]{0:T(512)S(1)} %bitcast.88, s32[512]{0:T(512)S(1)} %bitcast.83), kind=kOutput, calls=%fused_computation.9 | convolution fusion | flops 2284421120 | bytes 6557696 | tf_op jit(solution)/shard_map/dot_general | solution.py:21
  187.8 9.4 %fusion.20 = f32[4,272,2048]{2,1,0:T(8,128)} fusion(bf16[4,272,512]{2,1,0:T(8,128)(2,1)S(1)} %get-tuple-element.6, bf16[4,2048,512]{2,1,0:T(8,128)(2,1)} %param.11), kind=kOutput, calls=%fused_computation.58 | convolution fusion | flops 2281701376 | bytes 18415616 | tf_op jit(solution)/shard_map/erf,edf->erd/dot_general | solution.py:99
  197.2 0.8 copy-done.1
  197.9 3.6 %all-to-all-start.3 = ((bf16[4,4,32,2048]{3,2,1,0:T(8,128)(2,1)}), bf16[4,4,32,2048]{3,2,1,0:T(8,128)(2,1)S(1)}, u32[]{:S(2)}, u32[]{:S(2)}) async-start(bf16[4,4,32,2048]{3,2,1,0:T(8,128)(2,1)} %bitcast.73), calls=%async_computation.3 | async-start | bytes 4194304 | tf_op jit(solution)/shard_map/all_to_all | solution.py:50
  201.6 10.5 %add_convert_fusion = bf16[4,272,2048]{2,1,0:T(8,128)(2,1)} fusion(f32[4,272,2048]{2,1,0:T(8,128)} %fusion.20, bf16[4,272,512]{2,1,0:T(8,128)(2,1)S(1)} %get-tuple-element.5, bf16[4,2048,512]{2,1,0:T(8,128)(2,1)} %param.12), kind=kOutput, calls=%fused_computation.1 | convolution fusion | flops 2286157824 | bytes 22872064 | tf_op jit(solution)/shard_map/erf,edf->erd/dot_general | solution.py:99
  212.1 6.4 %convolution_convert_fusion.1 = bf16[512,2048]{1,0:T(8,128)(2,1)} fusion(bf16[1088,2048]{1,0:T(8,128)(2,1)} %bitcast.70, s32[512]{0:T(512)S(1)} %bitcast.89, s32[512]{0:T(512)S(1)} %bitcast.84), kind=kOutput, calls=%fused_computation.8 | convolution fusion | flops 2284421120 | bytes 6557696 | tf_op jit(solution)/shard_map/dot_general | solution.py:21
  218.5 7.4 %all-to-all-done.3 = bf16[4,4,32,2048]{3,2,1,0:T(8,128)(2,1)S(1)} async-done(((bf16[4,4,32,2048]{3,2,1,0:T(8,128)(2,1)}), bf16[4,4,32,2048]{3,2,1,0:T(8,128)(2,1)S(1)}, u32[]{:S(2)}, u32[]{:S(2)}) %all-to-all-start.3) | async-done | bytes 2097184 | tf_op jit(solution)/shard_map/all_to_all | solution.py:50
  225.9 1.3 copy-done
  227.2 3.8 %all-to-all-start.7 = ((bf16[4,4,32,2048]{3,2,1,0:T(8,128)(2,1)}), bf16[4,4,32,2048]{3,2,1,0:T(8,128)(2,1)S(1)}, u32[]{:S(2)}, u32[]{:S(2)}) async-start(bf16[4,4,32,2048]{3,2,1,0:T(8,128)(2,1)} %bitcast.71), calls=%async_computation.7 | async-start | bytes 4194304 | tf_op jit(solution)/shard_map/all_to_all | solution.py:50
  231.7 1.7 collective-permute-done.3
  233.4 1.3 broadcast_select_fusion.5
  234.9 8.1 %convert_bitcast_fusion.2 = bf16[1,2048,2048]{2,1,0:T(8,128)(2,1)} fusion(bf16[272,2048]{1,0:T(8,128)(2,1)S(1)} %bitcast.76, bf16[4,272,2048]{2,1,0:T(8,128)(2,1)} %bitcast.96, s32[]{:T(128)S(6)} %select_n.47), kind=kOutput, calls=%fused_computation.5 | convolution fusion | flops 2285895680 | bytes 10616836 | tf_op jit(solution)/shard_map/dot_general | solution.py:21
  243.0 2.9 %reduce_sum.68 = bf16[4,32,2048]{2,1,0:T(8,128)(2,1)} reduce(bf16[4,4,32,2048]{3,2,1,0:T(8,128)(2,1)} %copy-done, bf16[]{:T(256)} %constant.36.clone.1), dimensions={0}, to_apply=%region_2.3 | reduce | flops 786432 | bytes 2621442 | tf_op jit(solution)/shard_map/reduce_sum | solution.py:51
  245.9 9.2 %all-to-all-done.7 = bf16[4,4,32,2048]{3,2,1,0:T(8,128)(2,1)S(1)} async-done(((bf16[4,4,32,2048]{3,2,1,0:T(8,128)(2,1)}), bf16[4,4,32,2048]{3,2,1,0:T(8,128)(2,1)S(1)}, u32[]{:S(2)}, u32[]{:S(2)}) %all-to-all-start.7) | async-done | bytes 2097184 | tf_op jit(solution)/shard_map/all_to_all | solution.py:50
  255.1 4.8 %all-to-all-start.4 = ((bf16[4,32,2048]{2,1,0:T(8,128)(2,1)}), bf16[4,32,2048]{2,1,0:T(8,128)(2,1)}, u32[]{:S(2)}, u32[]{:S(2)}) async-start(bf16[4,32,2048]{2,1,0:T(8,128)(2,1)} %reduce_sum.68), calls=%async_computation.4 | async-start | bytes 1048576 | tf_op jit(solution)/shard_map/all_to_all | solution.py:50
  259.9 1.1 broadcast_select_fusion.3
  261.2 8.1 %convert_bitcast_fusion.1 = bf16[1,2048,2048]{2,1,0:T(8,128)(2,1)} fusion(bf16[272,2048]{1,0:T(8,128)(2,1)S(1)} %bitcast.75, bf16[4,272,2048]{2,1,0:T(8,128)(2,1)} %bitcast.97, s32[]{:T(128)S(6)} %select_n.47), kind=kOutput, calls=%fused_computation.4 | convolution fusion | flops 2285895680 | bytes 10616836 | tf_op jit(solution)/shard_map/dot_general | solution.py:21
  269.3 1.3 reduce_sum.70
  270.6 3.0 %all-to-all-done.4 = bf16[4,32,2048]{2,1,0:T(8,128)(2,1)} async-done(((bf16[4,32,2048]{2,1,0:T(8,128)(2,1)}), bf16[4,32,2048]{2,1,0:T(8,128)(2,1)}, u32[]{:S(2)}, u32[]{:S(2)}) %all-to-all-start.4) | async-done | bytes 524320 | tf_op jit(solution)/shard_map/all_to_all | solution.py:50
  273.6 3.5 %all-to-all-start.8 = ((bf16[4,32,2048]{2,1,0:T(8,128)(2,1)}), bf16[4,32,2048]{2,1,0:T(8,128)(2,1)S(1)}, u32[]{:S(2)}, u32[]{:S(2)}) async-start(bf16[4,32,2048]{2,1,0:T(8,128)(2,1)} %reduce_sum.70), calls=%async_computation.8 | async-start | bytes 1048576 | tf_op jit(solution)/shard_map/all_to_all | solution.py:50
  277.1 1.1 broadcast_select_fusion.1
  278.5 8.1 %convert_bitcast_fusion = bf16[1,2048,2048]{2,1,0:T(8,128)(2,1)} fusion(bf16[272,2048]{1,0:T(8,128)(2,1)S(1)} %bitcast.74, bf16[4,272,2048]{2,1,0:T(8,128)(2,1)} %bitcast.93, s32[]{:T(128)S(6)} %select_n.47), kind=kOutput, calls=%fused_computation.3 | convolution fusion | flops 2285895680 | bytes 10616836 | tf_op jit(solution)/shard_map/dot_general | solution.py:21
  286.5 1.8 reduce_sum.69
  288.3 2.7 all-to-all-done.8
  291.1 0.7 reduce_sum.71
  (55 shorter events, 2.7 us)
Async XLA Ops:
  0.6 23.2 %copy-start.9 = (bf16[28,2048]{1,0:T(8,128)(2,1)S(1)}, bf16[28,2048]{1,0:T(8,128)(2,1)}, u32[]{:S(2)}) copy-start(bf16[28,2048]{1,0:T(8,128)(2,1)} %param.7) | copy-start | bytes 344068
  4.0 15.5 %all-to-all-start = ((f32[16,1,128]{2,1,0:T(1,128)}), f32[16,1,128]{2,1,0:T(1,128)S(1)}, u32[]{:S(2)}, u32[]{:S(2)}) async-start(f32[16,1,128]{2,1,0:T(1,128)} %reshape.67), calls=%async_computation | async-start | bytes 16384 | tf_op jit(solution)/shard_map/all_to_all | solution.py:46
  20.4 16.8 %all-to-all-start.5 = ((bf16[4,32,2048]{2,1,0:T(8,128)(2,1)}), bf16[4,32,2048]{2,1,0:T(8,128)(2,1)S(1)}, u32[]{:S(2)}, u32[]{:S(2)}) async-start(bf16[4,32,2048]{2,1,0:T(8,128)(2,1)} %broadcast_in_dim.73), calls=%async_computation.5 | async-start | bytes 1048576 | tf_op jit(solution)/shard_map/all_to_all | solution.py:46
  55.0 27.5 %all-to-all-start.6 = ((bf16[4,4,32,2048]{3,2,1,0:T(8,128)(2,1)}), bf16[4,4,32,2048]{3,2,1,0:T(8,128)(2,1)S(1)}, u32[]{:S(2)}, u32[]{:S(2)}) async-start(bf16[4,4,32,2048]{3,2,1,0:T(8,128)(2,1)} %broadcast_in_dim.74), calls=%async_computation.6 | async-start | bytes 4194304 | tf_op jit(solution)/shard_map/all_to_all | solution.py:46
  84.1 28.9 %all-to-all-start.2 = ((bf16[4,4,32,2048]{3,2,1,0:T(8,128)(2,1)}), bf16[4,4,32,2048]{3,2,1,0:T(8,128)(2,1)}, u32[]{:S(2)}, u32[]{:S(2)}) async-start(bf16[4,4,32,2048]{3,2,1,0:T(8,128)(2,1)} %broadcast_in_dim.67), calls=%async_computation.2 | async-start | bytes 4194304 | tf_op jit(solution)/shard_map/all_to_all | solution.py:46
  91.7 7.5 %copy-start.10 = (bf16[1088,2048]{1,0:T(8,128)(2,1)}, bf16[1088,2048]{1,0:T(8,128)(2,1)S(1)}, u32[]{:S(2)}) copy-start(bf16[1088,2048]{1,0:T(8,128)(2,1)S(1)} %fusion) | copy-start | bytes 13369348
  99.2 18.1 %copy-start.6 = (bf16[4,272,512]{2,1,0:T(8,128)(2,1)}, bf16[4,272,512]{2,1,0:T(8,128)(2,1)S(1)}, u32[]{:S(2)}) copy-start(bf16[4,272,512]{2,1,0:T(8,128)(2,1)S(1)} %convolution_convert_fusion.3) | copy-start | bytes 3342340
  99.2 29.6 %collective-permute-start.2 = (bf16[4,272,512]{2,1,0:T(8,128)(2,1)S(1)}, bf16[4,272,512]{2,1,0:T(8,128)(2,1)S(1)}, u32[]{:S(2)}, u32[]{:S(2)}) collective-permute-start(bf16[4,272,512]{2,1,0:T(8,128)(2,1)S(1)} %convolution_convert_fusion.3), channel_id=1, source_target_pairs={{0,1},{1,0},{2,3},{3,2},{4,5},{5,4},{6,7},{7,6},{8,9},{9,8},{10,11... | collective-permute-start | bytes 3342344 | tf_op jit(solution)/shard_map/ppermute | solution.py:28
  113.0 11.9 %slice-start = ((s8[8388608]{0:T(1024)(128)(4,1)}), s8[4194304]{0:T(1024)(128)(4,1)S(1)}, s32[]{:S(2)}) async-start(s8[8388608]{0:T(1024)(128)(4,1)} %bitcast.68), calls=%async_computation.12 | async-start | bytes 8388608
  117.2 7.6 %copy-start.11 = (bf16[1088,2048]{1,0:T(8,128)(2,1)}, bf16[1088,2048]{1,0:T(8,128)(2,1)S(1)}, u32[]{:S(2)}) copy-start(bf16[1088,2048]{1,0:T(8,128)(2,1)S(1)} %convolution_convert_fusion) | copy-start | bytes 13369348
  117.2 7.6 %slice-start.1 = ((s8[8388608]{0:T(1024)(128)(4,1)}), s8[4194304]{0:T(1024)(128)(4,1)S(1)}, s32[]{:S(2)}) async-start(s8[8388608]{0:T(1024)(128)(4,1)} %bitcast.68), calls=%async_computation.13 | async-start | bytes 8388608
  124.8 3.6 %copy-start.8 = (bf16[4,272,512]{2,1,0:T(8,128)(2,1)}, bf16[4,272,512]{2,1,0:T(8,128)(2,1)S(1)}, u32[]{:S(2)}) copy-start(bf16[4,272,512]{2,1,0:T(8,128)(2,1)S(1)} %convolution_convert_fusion.5) | copy-start | bytes 3342340
  124.8 4.1 %collective-permute-start = (bf16[4,272,512]{2,1,0:T(8,128)(2,1)S(1)}, bf16[4,272,512]{2,1,0:T(8,128)(2,1)}, u32[]{:S(2)}, u32[]{:S(2)}) collective-permute-start(bf16[4,272,512]{2,1,0:T(8,128)(2,1)S(1)} %convolution_convert_fusion.5), channel_id=1, source_target_pairs={{0,1},{1,0},{2,3},{3,2},{4,5},{5,4},{6,7},{7,6},{8,9},{9,8},{10,11... | collective-permute-start | bytes 3342344 | tf_op jit(solution)/shard_map/ppermute | solution.py:28
  128.4 3.2 %collective-permute-start.1 = (bf16[4,272,512]{2,1,0:T(8,128)(2,1)}, bf16[4,272,512]{2,1,0:T(8,128)(2,1)}, u32[]{:S(2)}, u32[]{:S(2)}) collective-permute-start(bf16[4,272,512]{2,1,0:T(8,128)(2,1)} %convolution_convert_fusion.4), channel_id=1, source_target_pairs={{0,1},{1,0},{2,3},{3,2},{4,5},{5,4},{6,7},{7,6},{8,9},{9,8},{10,11... | collective-permute-start | bytes 3342344 | tf_op jit(solution)/shard_map/ppermute | solution.py:28
  128.8 1.0 copy-start.7
  138.2 19.5 %all-to-all-start.9 = ((bf16[4,272,256]{2,1,0:T(8,128)(2,1)}), bf16[4,272,256]{2,1,0:T(8,128)(2,1)S(1)}, u32[]{:S(2)}, u32[]{:S(2)}) async-start(bf16[4,272,256]{2,1,0:T(8,128)(2,1)} %constant_dynamic-slice_fusion.2), calls=%async_computation.9 | async-start | bytes 1114112 | tf_op jit(solution)/shard_map/all_to_all | solution.py:111
  157.6 0.8 copy-start.5
  158.4 18.6 %all-to-all-start.10 = ((bf16[4,272,256]{2,1,0:T(8,128)(2,1)}), bf16[4,272,256]{2,1,0:T(8,128)(2,1)S(1)}, u32[]{:S(2)}, u32[]{:S(2)}) async-start(bf16[4,272,256]{2,1,0:T(8,128)(2,1)} %constant_dynamic-slice_fusion.1), calls=%async_computation.10 | async-start | bytes 1114112 | tf_op jit(solution)/shard_map/all_to_all | solution.py:111
  177.1 0.8 copy-start.3
  177.9 19.3 %all-to-all-start.11 = ((bf16[4,272,256]{2,1,0:T(8,128)(2,1)}), bf16[4,272,256]{2,1,0:T(8,128)(2,1)S(1)}, u32[]{:S(2)}, u32[]{:S(2)}) async-start(bf16[4,272,256]{2,1,0:T(8,128)(2,1)} %constant_dynamic-slice_fusion), calls=%async_computation.11 | async-start | bytes 1114112 | tf_op jit(solution)/shard_map/all_to_all | solution.py:111
  197.1 0.8 copy-start.1
  197.9 28.0 %all-to-all-start.3 = ((bf16[4,4,32,2048]{3,2,1,0:T(8,128)(2,1)}), bf16[4,4,32,2048]{3,2,1,0:T(8,128)(2,1)S(1)}, u32[]{:S(2)}, u32[]{:S(2)}) async-start(bf16[4,4,32,2048]{3,2,1,0:T(8,128)(2,1)} %bitcast.73), calls=%async_computation.3 | async-start | bytes 4194304 | tf_op jit(solution)/shard_map/all_to_all | solution.py:50
  218.5 12.7 %copy-start.4 = (bf16[4,272,256]{2,1,0:T(8,128)(2,1)S(1)}, bf16[4,272,256]{2,1,0:T(8,128)(2,1)}, u32[]{:S(2)}) copy-start(bf16[4,272,256]{2,1,0:T(8,128)(2,1)} %copy-done.3) | copy-start | bytes 1671172
  218.5 13.2 %copy-start.2 = (bf16[4,272,256]{2,1,0:T(8,128)(2,1)S(1)}, bf16[4,272,256]{2,1,0:T(8,128)(2,1)}, u32[]{:S(2)}) copy-start(bf16[4,272,256]{2,1,0:T(8,128)(2,1)} %copy-done.1) | copy-start | bytes 1671172
  225.9 1.3 copy-start
  227.2 27.9 %all-to-all-start.7 = ((bf16[4,4,32,2048]{3,2,1,0:T(8,128)(2,1)}), bf16[4,4,32,2048]{3,2,1,0:T(8,128)(2,1)S(1)}, u32[]{:S(2)}, u32[]{:S(2)}) async-start(bf16[4,4,32,2048]{3,2,1,0:T(8,128)(2,1)} %bitcast.71), calls=%async_computation.7 | async-start | bytes 4194304 | tf_op jit(solution)/shard_map/all_to_all | solution.py:50
  231.1 2.4 collective-permute-start.3
  231.2 28.7 %collective-permute-start.4 = (bf16[4,272,256]{2,1,0:T(8,128)(2,1)S(1)}, bf16[4,272,256]{2,1,0:T(8,128)(2,1)}, u32[]{:S(2)}, u32[]{:S(2)}) collective-permute-start(bf16[4,272,256]{2,1,0:T(8,128)(2,1)S(1)} %copy-done.4), channel_id=1, source_target_pairs={{0,1},{1,0},{2,3},{3,2},{4,5},{5,4},{6,7},{7,6},{8,9},{9,8},{10,11... | collective-permute-start | bytes 1671176 | tf_op jit(solution)/shard_map/ppermute | solution.py:36
  231.6 45.5 %collective-permute-start.5 = (bf16[4,272,256]{2,1,0:T(8,128)(2,1)S(1)}, bf16[4,272,256]{2,1,0:T(8,128)(2,1)}, u32[]{:S(2)}, u32[]{:S(2)}) collective-permute-start(bf16[4,272,256]{2,1,0:T(8,128)(2,1)S(1)} %copy-done.2), channel_id=1, source_target_pairs={{0,1},{1,0},{2,3},{3,2},{4,5},{5,4},{6,7},{7,6},{8,9},{9,8},{10,11... | collective-permute-start | bytes 1671176 | tf_op jit(solution)/shard_map/ppermute | solution.py:36
  255.1 18.5 %all-to-all-start.4 = ((bf16[4,32,2048]{2,1,0:T(8,128)(2,1)}), bf16[4,32,2048]{2,1,0:T(8,128)(2,1)}, u32[]{:S(2)}, u32[]{:S(2)}) async-start(bf16[4,32,2048]{2,1,0:T(8,128)(2,1)} %reduce_sum.68), calls=%async_computation.4 | async-start | bytes 1048576 | tf_op jit(solution)/shard_map/all_to_all | solution.py:50
  273.6 17.4 %all-to-all-start.8 = ((bf16[4,32,2048]{2,1,0:T(8,128)(2,1)}), bf16[4,32,2048]{2,1,0:T(8,128)(2,1)S(1)}, u32[]{:S(2)}, u32[]{:S(2)}) async-start(bf16[4,32,2048]{2,1,0:T(8,128)(2,1)} %reduce_sum.70), calls=%async_computation.8 | async-start | bytes 1048576 | tf_op jit(solution)/shard_map/all_to_all | solution.py:50
